TPU v7x, 256 devices: a whole 4x4x8 slice. The times are simulated.
256 devices in a mesh: row: 32 (over y, z), col: 8 (over x, core).
Axes of the slice: x: 4, y: 4, z: 8, core: 2. Of those that a mesh axis runs over, the one named last changes fastest.
Arguments:
- tokens: bfloat16 [256, 16384], P('row', 'col'), may hold values from -6 to 6
- gate_frozen_weight: bfloat16 [16384, 28672], P('col', 'row'), may hold values from -0.046875 to 0.046875
- up_frozen_weight: bfloat16 [16384, 28672], P('col', 'row'), may hold values from -0.046875 to 0.046875
- down_frozen_weight: bfloat16 [28672, 16384], P('row', 'col'), may hold values from -0.03125 to 0.03125
- gate_adapter_squeeze: bfloat16 [16384, 16], P('col'), may hold values from -0.046875 to 0.046875
- gate_adapter_lift: bfloat16 [16, 28672], P(None, 'row'), may hold values from -1.5 to 1.5
- up_adapter_squeeze: bfloat16 [16384, 16], P('col'), may hold values from -0.046875 to 0.046875
- up_adapter_lift: bfloat16 [16, 28672], P(None, 'row'), may hold values from -1.5 to 1.5
- down_adapter_squeeze: bfloat16 [28672, 16], P('row'), may hold values from -0.03125 to 0.03125
- down_adapter_lift: bfloat16 [16, 16384], P(None, 'col'), may hold values from -1.5 to 1.5
- output_gradient: bfloat16 [256, 16384], P('row', 'col'), may hold values from -6 to 6
Outputs:
- mixed: bfloat16 [256, 16384], P('row', 'col')
- token_gradient: bfloat16 [256, 16384], P('row', 'col')
All inputs are finite; a program needn't handle non-finite values.
Results may differ from a plain program's by a relative error of at most 0.005.
Values may be sent and summed in bfloat16 or wider, within the bound.
A program may use at most 64 MiB of HBM per device.

v0:
```python
import jax
import jax.numpy as jnp
from jax import lax
from jax.sharding import PartitionSpec as P

ADAPTER_SCALE = 0.5


def contract_last(left, right):
    return lax.dot_general(
        left, right, (((1,), (1,)), ((), ())), preferred_element_type=jnp.float32
    )


def precise_contract_trailing(left, right):
    return lax.dot_general(
        left, right.astype(jnp.float32), (((1,), (1,)), ((), ())), precision=lax.Precision.HIGHEST
    )


def precise_matmul(left, right):
    return jnp.dot(left, right.astype(jnp.float32), precision=lax.Precision.HIGHEST)


def on_device(
    tokens,
    gate_frozen_weight,
    up_frozen_weight,
    down_frozen_weight,
    gate_adapter_squeeze,
    gate_adapter_lift,
    up_adapter_squeeze,
    up_adapter_lift,
    down_adapter_squeeze,
    down_adapter_lift,
    output_gradient,
):
    row_count = tokens.shape[0]
    leading_column = (lax.axis_index("col") == 0).astype(jnp.float32)
    own_begin = lax.axis_index("row") * row_count
    token_panel = lax.all_gather(tokens, "row", axis=0, tiled=True)
    gate_portion = jnp.dot(token_panel, gate_frozen_weight, preferred_element_type=jnp.float32)
    up_portion = jnp.dot(token_panel, up_frozen_weight, preferred_element_type=jnp.float32)
    gate_rank_inner = jnp.dot(token_panel, gate_adapter_squeeze, preferred_element_type=jnp.float32)
    up_rank_inner = jnp.dot(token_panel, up_adapter_squeeze, preferred_element_type=jnp.float32)
    gate_rank_inner, up_rank_inner = lax.psum((gate_rank_inner, up_rank_inner), "col")
    gate_portion = gate_portion + leading_column * ADAPTER_SCALE * precise_matmul(
        gate_rank_inner, gate_adapter_lift
    )
    up_portion = up_portion + leading_column * ADAPTER_SCALE * precise_matmul(
        up_rank_inner, up_adapter_lift
    )
    gate_complete, up_complete = lax.psum((gate_portion, up_portion), "col")
    sigmoid_gate = jax.nn.sigmoid(gate_complete)
    hidden_activation = (gate_complete * sigmoid_gate * up_complete).astype(jnp.bfloat16)
    term = jnp.dot(hidden_activation, down_frozen_weight, preferred_element_type=jnp.float32)
    combined_total = lax.psum_scatter(term, "row", scatter_dimension=0, tiled=True)
    down_inner = lax.psum(
        jnp.dot(hidden_activation, down_adapter_squeeze, preferred_element_type=jnp.float32), "row"
    )
    local_rank_inner = lax.dynamic_slice_in_dim(down_inner, own_begin, row_count, 0)
    combined_total = combined_total + ADAPTER_SCALE * precise_matmul(
        local_rank_inner, down_adapter_lift
    )
    mixed = combined_total.astype(jnp.bfloat16)
    cotangent_panel = lax.all_gather(output_gradient, "row", axis=0, tiled=True)
    portion_gradient = contract_last(cotangent_panel, down_frozen_weight)
    inner_gradient = contract_last(cotangent_panel, down_adapter_lift)
    inner_gradient = lax.psum(inner_gradient, "col")
    portion_gradient = (
        portion_gradient
        + leading_column
        * ADAPTER_SCALE
        * precise_contract_trailing(inner_gradient, down_adapter_squeeze)
    )
    hidden_gradient = lax.psum(portion_gradient, "col")
    gate_gradient = (
        hidden_gradient * up_complete * sigmoid_gate * (1.0 + gate_complete * (1.0 - sigmoid_gate))
    ).astype(jnp.bfloat16)
    up_gradient = (hidden_gradient * gate_complete * sigmoid_gate).astype(jnp.bfloat16)
    term = contract_last(gate_gradient, gate_frozen_weight) + contract_last(
        up_gradient, up_frozen_weight
    )
    input_total = lax.psum_scatter(term, "row", scatter_dimension=0, tiled=True)
    gate_back, up_back = lax.psum(
        (
            contract_last(gate_gradient, gate_adapter_lift),
            contract_last(up_gradient, up_adapter_lift),
        ),
        "row",
    )
    own_gate = lax.dynamic_slice_in_dim(gate_back, own_begin, row_count, 0)
    own_up = lax.dynamic_slice_in_dim(up_back, own_begin, row_count, 0)
    input_total = input_total + ADAPTER_SCALE * (
        precise_contract_trailing(own_gate, gate_adapter_squeeze)
        + precise_contract_trailing(own_up, up_adapter_squeeze)
    )
    return (mixed, input_total.astype(jnp.bfloat16))


def solution(mesh):
    placed = (
        P("row", "col"),
        P("col", "row"),
        P("col", "row"),
        P("row", "col"),
        P("col", None),
        P(None, "row"),
        P("col", None),
        P(None, "row"),
        P("row", None),
        P(None, "col"),
        P("row", "col"),
    )
    return jax.shard_map(
        on_device,
        mesh=mesh,
        in_specs=placed,
        out_specs=(P("row", "col"), P("row", "col")),
        check_vma=False,
    )
```

profile of v0, /device:TPU:32, one launch (start us, length us, event | category | flops | bytes accessed | tf_op | source)
XLA Modules:
  0.0 722.1 jit_solution(16278052641499378771)
XLA Ops:
  7.2 0.0 copy-start
  7.2 0.0 all-gather.3.cloned.1.call-start
  7.2 0.7 all-gather.3.cloned.1.call-update
  7.9 0.0 all-gather.5.cloned.1.call-start
  8.0 0.7 all-gather.5.cloned.1.call-update
  8.7 0.0 all-reduce.5.cloned.1.call-start
  8.7 79.7 %all-gather.3.cloned.1.call-done = bf16[256,2048]{1,0:T(8,128)(2,1)} async-done(((bf16[8,2048]{1,0:T(8,128)(2,1)}), bf16[256,2048]{1,0:T(8,128)(2,1)}) %all-gather.3.cloned.1.call-update) | async-done | bytes 1048592 | tf_op jit(solution)/shard_map/all_gather | solution.py:41
  88.5 1.6 fusion.18
  90.1 0.0 copy-done
  90.1 1.6 fusion.16
  91.8 73.1 %all-gather.5.cloned.1.call-done = bf16[256,2048]{1,0:T(8,128)(2,1)} async-done(((bf16[8,2048]{1,0:T(8,128)(2,1)}), bf16[256,2048]{1,0:T(8,128)(2,1)}) %all-gather.5.cloned.1.call-update) | async-done | bytes 1048592 | tf_op jit(solution)/shard_map/all_gather | solution.py:66
  164.9 1.6 fusion.22
  166.5 0.0 copy-start.10
  166.5 27.7 %all-reduce.1 = (f32[256,16]{1,0:T(8,128)S(1)}, f32[256,16]{1,0:T(8,128)S(1)}, f32[256,16]{1,0:T(8,128)S(1)}) all-reduce(f32[256,16]{1,0:T(8,128)S(1)} %fusion.18, f32[256,16]{1,0:T(8,128)S(1)} %fusion.16, f32[256,16]{1,0:T(8,128)S(1)} %fusion.22), channel_id=1, replica_groups=mesh['row'=32,'col'=8] {'col'}, use_global_device_ids=true, to_apply=%region_2.0 | all-reduce | flops 12288 | bytes 98304 | tf_op jit(solution)/shard_map/psum | solution.py:46
  194.2 0.0 copy-start.1
  194.2 0.0 copy-start.3
  194.3 3.8 fusion.21
  198.0 0.0 copy-done.10
  198.1 1.4 fusion.5
  199.5 0.0 copy-done.1
  199.5 0.0 copy-done.3
  199.5 0.0 copy-start.9
  199.5 0.0 copy-start.4
  199.5 1.3 fusion.15
  200.8 0.0 copy-done.9
  200.8 1.5 fusion.7
  202.3 0.0 copy-done.4
  202.3 0.0 copy-start.8
  202.3 1.3 fusion.17
  203.6 0.0 copy-done.8
  203.6 1.5 fusion.6
  205.1 0.0 all-reduce.5.cloned.1.call-update
  205.1 0.0 reduce-scatter.3.cloned.1.call-start
  205.1 69.3 %all-reduce.5.cloned.1.call-done = (f32[256,896]{1,0:T(8,128)}, f32[256,896]{1,0:T(8,128)}, f32[256,896]{1,0:T(8,128)}) async-done(((f32[256,896]{1,0:T(8,128)}, f32[256,896]{1,0:T(8,128)}, f32[256,896]{1,0:T(8,128)}), (f32[256,896]{1,0:T(8,128)}, f32[256,896]{1,0:T(8,128)}, f32[256,896]{1,0:T(8,128)})) %all-reduce.5.cloned.1.call-update) | async-done | bytes 2752528 | tf_op jit(solution)/shard_map/psum | solution.py:53
  274.4 0.0 copy-start.2
  274.4 2.4 multiply_convert_fusion
  276.8 0.5 copy-done.2
  277.3 2.6 fusion.19
  279.9 0.0 reduce-scatter.3.cloned.1.call-update
  279.9 0.0 reduce-scatter.5.cloned.1.call-start
  280.0 0.0 copy-start.5
  280.0 3.5 fusion.23
  283.5 0.0 copy-done.5
  283.5 2.6 convolution_add_fusion
  286.1 0.0 copy-start.7
  286.1 0.0 copy-start.6
  286.1 0.0 reduce-scatter.5.cloned.1.call-update
  286.1 0.2 fusion.25
  286.4 0.2 fusion.24
  286.6 0.2 fusion.20
  286.9 141.7 %all-reduce = (f32[256,16]{1,0:T(8,128)S(1)}, f32[256,16]{1,0:T(8,128)S(1)}, f32[256,16]{1,0:T(8,128)S(1)}) all-reduce(f32[256,16]{1,0:T(8,128)S(1)} %fusion.20, f32[256,16]{1,0:T(8,128)S(1)} %fusion.24, f32[256,16]{1,0:T(8,128)S(1)} %fusion.25), channel_id=1, replica_groups=mesh['row'=32,'col'=8] {'row'}, use_global_device_ids=true, to_apply=%region_5.0 | all-reduce | flops 12288 | bytes 98304 | tf_op jit(solution)/shard_map/psum | solution.py:58
  428.6 0.2 fusion.9
  428.8 66.8 %reduce-scatter.3.cloned.1.call-done = f32[8,2048]{1,0:T(8,128)} async-done(((f32[256,2048]{1,0:T(8,128)}), f32[8,2048]{1,0:T(8,128)}) %reduce-scatter.3.cloned.1.call-update) | async-done | bytes 65552 | tf_op jit(solution)/shard_map/reduce_scatter | solution.py:57
  495.6 0.0 copy-done.7
  495.6 1.6 fusion.3
  497.2 216.7 %reduce-scatter.5.cloned.1.call-done = f32[8,2048]{1,0:T(8,128)} async-done(((f32[256,2048]{1,0:T(8,128)}), f32[8,2048]{1,0:T(8,128)}) %reduce-scatter.5.cloned.1.call-update) | async-done | bytes 65552 | tf_op jit(solution)/shard_map/reduce_scatter | solution.py:84
  714.0 0.0 copy-done.6
  714.0 1.6 fusion.4
Async XLA Ops:
  7.2 82.9 %copy-start = (bf16[2048,16]{0,1:T(8,128)(2,1)S(1)}, bf16[2048,16]{0,1:T(8,128)(2,1)}, u32[]{:S(2)}) copy-start(bf16[2048,16]{0,1:T(8,128)(2,1)} %param.15) | copy-start | bytes 196612
  7.2 81.3 %all-gather.3.cloned.1.call-start = ((), (), s32[]{:S(2)}) async-start(), calls=%async_computation.2 | async-start | bytes 1081344 | tf_op jit(solution)/shard_map/all_gather | solution.py:41
  7.9 157.0 %all-gather.5.cloned.1.call-start = ((), (), s32[]{:S(2)}) async-start(), calls=%async_computation.4 | async-start | bytes 1081344 | tf_op jit(solution)/shard_map/all_gather | solution.py:66
  8.7 265.7 %all-reduce.5.cloned.1.call-start = ((), (), s32[]{:S(2)}) async-start(), calls=%async_computation.6 | async-start | bytes 5505024 | tf_op jit(solution)/shard_map/psum | solution.py:53
  166.5 31.5 %copy-start.10 = (bf16[896,16]{0,1:T(8,128)(2,1)S(1)}, bf16[896,16]{0,1:T(8,128)(2,1)}, u32[]{:S(2)}) copy-start(bf16[896,16]{0,1:T(8,128)(2,1)} %param.19) | copy-start | bytes 86020
  194.2 5.3 copy-start.1
  194.2 5.3 copy-start.3
  199.5 1.3 copy-start.9
  199.5 2.8 copy-start.4
  202.3 1.3 copy-start.8
  205.1 290.5 %reduce-scatter.3.cloned.1.call-start = ((), (), s32[]{:S(2)}) async-start(), calls=%async_computation.3 | async-start | bytes 2162688 | tf_op jit(solution)/shard_map/reduce_scatter | solution.py:57
  274.4 2.9 copy-start.2
  279.9 434.1 %reduce-scatter.5.cloned.1.call-start = ((), (), s32[]{:S(2)}) async-start(), calls=%async_computation.5 | async-start | bytes 2162688 | tf_op jit(solution)/shard_map/reduce_scatter | solution.py:84
  280.0 3.5 copy-start.5
  286.1 209.5 %copy-start.7 = (bf16[16,2048]{1,0:T(8,128)(2,1)S(1)}, bf16[16,2048]{1,0:T(8,128)(2,1)}, u32[]{:S(2)}) copy-start(bf16[16,2048]{1,0:T(8,128)(2,1)} %param.20) | copy-start | bytes 196612
  286.1 427.9 %copy-start.6 = (bf16[2048,16]{0,1:T(8,128)(2,1)S(1)}, bf16[2048,16]{0,1:T(8,128)(2,1)}, u32[]{:S(2)}) copy-start(bf16[2048,16]{0,1:T(8,128)(2,1)} %param.17) | copy-start | bytes 196612
Sparse Core Ops, SparseCore 0:
  10.6 77.8 all-gather.2
  91.1 73.7 all-gather.4
  205.2 69.1 all-reduce.4
  280.0 215.5 reduce-scatter.2
  499.3 214.6 reduce-scatter.4
where the time goes:
time: 724 us; the launch traced here: 722 us
  waiting for transfers between devices  507 us (70%)
  blocking collectives  169 us (23%)
  matrix products  28.5 us (4%)
  between operations  14 us (2%)
    reduce_scatter x1, waiting for transfers between devices, on_device(): input_total = lax.psum_scatter(term, 'row', scatter_dimension=0, tiled=True)  217 us
    psum x1, blocking collectives, on_device(): lax.psum(jnp.dot(hidden_activation, down_adapter_squeeze, preferred_eleme...  142 us
    all_gather x1, waiting for transfers between devices, on_device(): token_panel = lax.all_gather(tokens, 'row', axis=0, tiled=True)  79.7 us
    all_gather x1, waiting for transfers between devices, on_device(): cotangent_panel = lax.all_gather(output_gradient, 'row', axis=0, tiled=True)  73.1 us
    psum x1, waiting for transfers between devices, on_device(): gate_complete, up_complete = lax.psum((gate_portion, up_portion), 'col')  69.3 us
    reduce_scatter x1, waiting for transfers between devices, on_device(): lax.psum_scatter(term, 'row', scatter_dimension=0, tiled=True)  66.8 us
    psum x1, blocking collectives, on_device(): lax.psum((gate_rank_inner, up_rank_inner), 'col')  27.7 us
  transfers between devices with their start and end apart: 5, of which 5 were waited for; matrix products, arithmetic and copies ran while one was open for 2% of the time, Pallas kernels for 0%

commit v1 on v0

v1 whole, which is shorter than its diff:
```python
import jax
import jax.numpy as jnp
from jax import lax
from jax.experimental import pallas as pl
from jax.experimental.pallas import tpu as pltpu
from jax.sharding import PartitionSpec as P

MESH = pl.DeviceIdType.MESH
F32, BF16 = jnp.float32, jnp.bfloat16

NX, NCORE, NY, NZ = 4, 2, 4, 8
T, DC, FR, RANK = 256, 2048, 896, 16
FA = 1024
HALF, QUART = T // NCORE, T // NCORE // NX
TY = T // NY
CW = 512
NCH = DC // CW
ZORD = (1, 7, 2, 6, 3, 5, 4)
YORD = (1, 3, 2)
SCALE = 0.5


def nn(a, b):
    return jnp.dot(a, b, preferred_element_type=F32)


def nt(a, b):
    return lax.dot_general(a, b, (((1,), (1,)), ((), ())), preferred_element_type=F32)


def split_inner(inner):
    top = inner.astype(BF16).astype(F32)
    lane = lax.broadcasted_iota(jnp.int32, inner.shape, 1)
    return (jnp.where(lane < RANK, top, inner - top) * SCALE).astype(BF16)


def kernel(
    x_ref, dy_ref, wg_ref, wu_ref, wd_ref, sg_ref, lg_ref, su_ref, lu_ref, sd_ref, ld_ref,
    mixed_ref, tg_ref,
    wga, wua, wda, lga, lua, sda, sgt, sut, sdt,
    g, pan, part, sib, own, xs, xr, act, mf, ms, ry, zo, zs, zr,
    wsem, ss, rs,
):
    r, c = lax.axis_index("row"), lax.axis_index("col")
    y, z = r // NZ, r % NZ
    x, k = c // NCORE, c % NCORE

    def dev(dx=0, dk=0, dy=0, dz=0):
        return {
            "row": ((y + dy) % NY) * NZ + (z + dz) % NZ,
            "col": ((x + dx) % NX) * NCORE + (k + dk) % NCORE,
        }

    peers = (
        [dict(dz=d) for d in range(1, NZ)]
        + [dict(dy=d) for d in range(1, NY)]
        + [dict(dx=d) for d in range(1, NX)]
        + [dict(dk=1)]
    )
    barrier = pltpu.get_barrier_semaphore()
    for p in peers:
        pl.semaphore_signal(barrier, inc=1, device_id=dev(**p), device_id_type=MESH)

    loads = {}

    def load(name, i, src, dst):
        cp = pltpu.make_async_copy(src, dst, wsem.at[i])
        cp.start()
        loads[name] = cp

    load("sg", 0, sg_ref, sgt)
    load("su", 1, su_ref, sut)
    load("wg", 2, wg_ref, wga.at[:, 0:FR])
    load("wu", 3, wu_ref, wua.at[:, 0:FR])
    load("lg0", 4, lg_ref, lga.at[0:RANK])
    load("lg1", 5, lg_ref, lga.at[RANK : 2 * RANK])
    load("lu0", 6, lu_ref, lua.at[0:RANK])
    load("lu1", 7, lu_ref, lua.at[RANK : 2 * RANK])
    load("wd", 8, wd_ref, wda.at[0:FR])
    load("ld0", 9, ld_ref, wda.at[FR : FR + RANK])
    load("ld1", 10, ld_ref, wda.at[FR + RANK : FR + 2 * RANK])
    load("sd", 11, sd_ref, sdt)

    for a, ref in enumerate((x_ref, dy_ref)):
        v = ref[...].astype(F32)
        g[a, r] = jnp.concatenate([v[:, : DC // 2], v[:, DC // 2 :]], axis=0).astype(BF16)

    pl.semaphore_wait(barrier, len(peers))

    started = []
    sems = {}

    def rsem(key):
        if key not in sems:
            sems[key] = len(sems)
        return rs.at[sems[key]]

    def send(src, dst, key, **to):
        cp = pltpu.make_async_remote_copy(
            src_ref=src, dst_ref=dst, send_sem=ss.at[len(started)], recv_sem=rsem(key),
            device_id=dev(**to), device_id_type=MESH,
        )
        cp.start()
        started.append(cp)

    def arrived(dst, key):
        pltpu.make_async_remote_copy(
            src_ref=dst, dst_ref=dst, send_sem=ss.at[0], recv_sem=rsem(key),
            device_id=dev(dk=1), device_id_type=MESH,
        ).wait_recv()

    def block(a, dy, dz):
        return g.at[a, ((y + dy) % NY) * NZ + (z + dz) % NZ]

    def gather_z(a):
        for dz in ZORD:
            send(block(a, 0, 0), block(a, 0, 0), ("gz", a, dz), dz=dz)

    def gather_y(a):
        for dz in (0,) + ZORD:
            b = block(a, 0, -dz)
            if dz:
                arrived(b, ("gz", a, dz))
            for dy in (1, 3):
                send(b, b, ("gy", a, dy, dz), dy=dy)

    def gather_forward(a, dzs):
        for dz in dzs:
            for dy, cols in ((1, slice(0, DC // 4)), (3, slice(DC // 4, DC // 2))):
                b = block(a, -dy, -dz)
                arrived(b, ("gy", a, dy, dz))
                send(b.at[:, cols], b.at[:, cols], ("gf", a, dy, dz), dy=dy)

    def gather_end(a):
        for dz in (0,) + ZORD:
            b = block(a, 2, -dz)
            arrived(b.at[:, 0 : DC // 4], ("gf", a, 1, dz))
            arrived(b.at[:, DC // 4 : DC // 2], ("gf", a, 3, dz))
        for i in range(8):
            v = g[a, 4 * i : 4 * i + 4].astype(F32).reshape(4, 2, 8, DC // 2)
            rows = slice(32 * i, 32 * i + 32)
            pan[a, rows, 0 : DC // 2] = v[:, 0].reshape(32, DC // 2).astype(BF16)
            pan[a, rows, DC // 2 : DC] = v[:, 1].reshape(32, DC // 2).astype(BF16)

    gather_z(0)
    gather_z(1)

    rows16 = lax.broadcasted_iota(jnp.int32, (RANK, 128), 0)
    lanes = lax.broadcasted_iota(jnp.int32, (RANK, 128), 1)
    twice = ((lanes % RANK == rows16) & (lanes < 2 * RANK)).astype(F32).astype(BF16)
    for name, src, dst in (("sg", sgt, wga), ("su", sut, wua)):
        loads[name].wait()
        dst[:, FR:FA] = nn(src[...], twice).astype(BF16)
    for dst in (lga, lua):
        dst[2 * RANK : 128] = jnp.zeros((128 - 2 * RANK, FR), BF16)
    wda[FR + 2 * RANK : FA] = jnp.zeros((FA - FR - 2 * RANK, DC), BF16)

    gather_y(0)
    loads["sd"].wait()
    sda[...] = nn(sdt[...], twice).astype(BF16)
    gather_forward(0, (0,) + ZORD)
    gather_y(1)
    for name in ("wg", "wu", "lg0", "lg1", "lu0", "lu1"):
        loads[name].wait()
    gather_end(0)

    other = pl.multiple_of((1 - k) * HALF, HALF)
    mine = pl.multiple_of(k * HALF, HALF)
    myrow = pl.multiple_of(k * HALF + x * QUART, QUART)

    def sum_cores(a):
        send(part.at[a, pl.ds(other, HALF)], sib.at[a], ("sib", a), dk=1)

    def sum_x(a):
        arrived(sib.at[a], ("sib", a))
        for q in range(NX):
            rows = pl.ds(pl.multiple_of(mine + q * QUART, QUART), QUART)
            v = part[a, rows, :] + sib[a, q * QUART : (q + 1) * QUART, :]
            own[a, q] = v
            xs[a, q] = v.astype(BF16)
        for dx in (1, 3, 2):
            send(xs.at[a, (x + dx) % NX], xr.at[a, dx - 1], ("xr", a, dx), dx=dx)

    def total_x(a):
        for dx in (1, 3, 2):
            arrived(xr.at[a, dx - 1], ("xr", a, dx))
        return own[a, x] + xr[a, 0].astype(F32) + xr[a, 1].astype(F32) + xr[a, 2].astype(F32)

    def forward_part(a, w, lift):
        o = nn(pan[0], w[:, 768:FA])
        sel = split_inner(o[:, 128:256])
        part[a, :, 768:FR] = o[:, 0:128] + nn(sel, lift[:, 768:FR])
        for j in range(3):
            cols = slice(256 * j, 256 * (j + 1))
            part[a, :, cols] = nn(pan[0], w[:, cols]) + nn(sel, lift[:, cols])

    forward_part(0, wga, lga)
    sum_cores(0)
    forward_part(1, wua, lua)
    sum_cores(1)
    sum_x(0)
    sum_x(1)
    gather_forward(1, (0,) + ZORD)

    def spread(a):
        b = act.at[a, pl.ds(myrow, QUART), 0:FR]
        for dx in (1, 3, 2):
            send(b, b, ("ax", a, dx), dx=dx)
        send(b, b, ("ak", a, 0), dk=1)

    def spread_on(a):
        for dx in (1, 3, 2):
            rows = pl.multiple_of(k * HALF + ((x - dx) % NX) * QUART, QUART)
            b = act.at[a, pl.ds(rows, QUART), 0:FR]
            arrived(b, ("ax", a, dx))
            send(b, b, ("ak", a, dx), dk=1)

    def spread_end(a):
        for dx in (0, 1, 3, 2):
            rows = pl.multiple_of((1 - k) * HALF + ((x - dx) % NX) * QUART, QUART)
            arrived(act.at[a, pl.ds(rows, QUART), 0:FR], ("ak", a, dx))

    gate = total_x(0)
    up = total_x(1)
    sigmoid = jax.nn.sigmoid(gate)
    act[0, pl.ds(myrow, QUART), 0:FR] = (gate * sigmoid * up).astype(BF16)
    spread(0)
    own[0, x] = gate
    own[1, x] = up

    for name in ("wd", "ld0", "ld1"):
        loads[name].wait()
    gather_end(1)
    spread_on(0)
    o = nt(pan[1], wda[768:FA, :])
    sel = split_inner(o[:, 128:256])
    part[2, :, 768:FR] = o[:, 0:128] + nt(sel, sda[768:FR, :])
    for j in range(3):
        cols = slice(256 * j, 256 * (j + 1))
        part[2, :, cols] = nt(pan[1], wda[cols, :]) + nt(sel, sda[cols, :])
    sum_cores(2)

    def y_send(a, j, value):
        cols = slice(CW * j, CW * (j + 1))
        mf[a, :, cols] = value
        ms[a, :, cols] = value.astype(BF16)
        for dy in YORD:
            rows = pl.multiple_of(((y + dy) % NY) * TY, TY)
            send(ms.at[a, pl.ds(rows, TY), cols], ry.at[a, dy - 1, :, cols], ("ry", a, j, dy), dy=dy)

    def z_send(a, j):
        cols = slice(CW * j, CW * (j + 1))
        for dy in YORD:
            arrived(ry.at[a, dy - 1, :, cols], ("ry", a, j, dy))
        v = mf[a, pl.ds(pl.multiple_of(y * TY, TY), TY), cols]
        for dy in YORD:
            v = v + ry[a, dy - 1, :, cols].astype(F32)
        zo[a, :, cols] = v
        if j % 2 == 0:
            return
        first = zo[a, :, CW * (j - 1) : CW * j].reshape(NZ, 8, CW)
        zs[a, j // 2] = jnp.concatenate([first, v.reshape(NZ, 8, CW)], axis=1).astype(BF16)
        for dz in ZORD:
            send(zs.at[a, j // 2, (z + dz) % NZ], zr.at[a, j // 2, dz - 1], ("zr", a, j // 2, dz), dz=dz)

    def z_end(a, out_ref):
        for h in range(NCH // 2):
            v = zo[a, pl.ds(pl.multiple_of(z * 8, 8), 8), 2 * CW * h : 2 * CW * (h + 1)]
            v = jnp.concatenate([v[:, :CW], v[:, CW:]], axis=0)
            for dz in ZORD:
                arrived(zr.at[a, h, dz - 1], ("zr", a, h, dz))
            for dz in ZORD:
                v = v + zr[a, h, dz - 1].astype(F32)
            out_ref[:, 2 * CW * h : 2 * CW * h + CW] = v[0:8].astype(BF16)
            out_ref[:, 2 * CW * h + CW : 2 * CW * (h + 1)] = v[8:16].astype(BF16)

    def down(j):
        y_send(0, j, nn(act[0], wda[:, CW * j : CW * (j + 1)]))

    def back(j):
        rows = slice(CW * j, CW * (j + 1))
        y_send(1, j, nt(act[1], wga[rows, :]) + nt(act[2], wua[rows, :]))

    spread_end(0)
    act[0, :, FR:FA] = split_inner(nn(act[0, :, 0:FR], sda[...]))
    down(0)
    sum_x(2)
    down(1)
    down(2)
    down(3)

    hidden_gradient = total_x(2)
    gate = own[0, x]
    up = own[1, x]
    sigmoid = jax.nn.sigmoid(gate)
    act[1, pl.ds(myrow, QUART), 0:FR] = (
        hidden_gradient * up * sigmoid * (1.0 + gate * (1.0 - sigmoid))
    ).astype(BF16)
    act[2, pl.ds(myrow, QUART), 0:FR] = (hidden_gradient * gate * sigmoid).astype(BF16)
    spread(1)
    spread(2)
    z_send(0, 0)
    spread_on(1)
    spread_on(2)
    z_send(0, 1)
    spread_end(1)
    act[1, :, FR:FA] = split_inner(nt(act[1, :, 0:FR], lga[...]))
    spread_end(2)
    act[2, :, FR:FA] = split_inner(nt(act[2, :, 0:FR], lua[...]))
    back(0)
    z_send(0, 2)
    back(1)
    z_send(0, 3)
    back(2)
    back(3)
    z_send(1, 0)
    z_send(1, 1)
    z_end(0, mixed_ref)
    z_send(1, 2)
    z_send(1, 3)
    z_end(1, tg_ref)
    for cp in started:
        cp.wait_send()


def on_device(tokens, gate_w, up_w, down_w, gate_s, gate_l, up_s, up_l, down_s, down_l, cotangent):
    vmem = pl.BlockSpec(memory_space=pltpu.VMEM)
    anywhere = pl.BlockSpec(memory_space=pl.ANY)
    out = jax.ShapeDtypeStruct((T // NY // NZ, DC), BF16)
    return pl.pallas_call(
        kernel,
        out_shape=(out, out),
        in_specs=[vmem] * 2 + [anywhere] * 9,
        out_specs=(vmem, vmem),
        scratch_shapes=[
            pltpu.VMEM((DC, FA), BF16),
            pltpu.VMEM((DC, FA), BF16),
            pltpu.VMEM((FA, DC), BF16),
            pltpu.VMEM((128, FR), BF16),
            pltpu.VMEM((128, FR), BF16),
            pltpu.VMEM((FR, 128), BF16),
            pltpu.VMEM((DC, RANK), BF16),
            pltpu.VMEM((DC, RANK), BF16),
            pltpu.VMEM((FR, RANK), BF16),
            pltpu.VMEM((2, NY * NZ, 16, DC // 2), BF16),
            pltpu.VMEM((2, T, DC), BF16),
            pltpu.VMEM((3, T, FR), F32),
            pltpu.VMEM((3, HALF, FR), F32),
            pltpu.VMEM((3, NX, QUART, FR), F32),
            pltpu.VMEM((3, NX, QUART, FR), BF16),
            pltpu.VMEM((3, NX - 1, QUART, FR), BF16),
            pltpu.VMEM((3, T, FA), BF16),
            pltpu.VMEM((2, T, DC), F32),
            pltpu.VMEM((2, T, DC), BF16),
            pltpu.VMEM((2, NY - 1, TY, DC), BF16),
            pltpu.VMEM((2, TY, DC), F32),
            pltpu.VMEM((2, NCH // 2, NZ, 16, CW), BF16),
            pltpu.VMEM((2, NCH // 2, NZ - 1, 16, CW), BF16),
            pltpu.SemaphoreType.DMA((12,)),
            pltpu.SemaphoreType.DMA((200,)),
            pltpu.SemaphoreType.DMA((200,)),
        ],
        compiler_params=pltpu.CompilerParams(
            collective_id=0, has_side_effects=True, vmem_limit_bytes=58 * 2**20
        ),
        name="lora_swiglu",
    )(tokens, cotangent, gate_w, up_w, down_w, gate_s, gate_l, up_s, up_l, down_s, down_l)


def solution(mesh):
    placed = (
        P("row", "col"),
        P("col", "row"),
        P("col", "row"),
        P("row", "col"),
        P("col", None),
        P(None, "row"),
        P("col", None),
        P(None, "row"),
        P("row", None),
        P(None, "col"),
        P("row", "col"),
    )
    return jax.shard_map(
        on_device,
        mesh=mesh,
        in_specs=placed,
        out_specs=(P("row", "col"), P("row", "col")),
        check_vma=False,
    )
```

time: 724 us -> 95.5 us (0.13)
  waiting for transfers between devices: 507 us -> 0 us
  blocking collectives: 169 us -> 0 us
  Pallas kernels: 0 us -> 86.4 us
  matrix products: 28.5 us -> 0 us
  between operations: 14 us -> 0.64 us
  local copies, waits for them, and re-layouts: 0.52 us -> 8.03 us
    reduce_scatter x2 -> x0, waiting for transfers between devices: 284 us -> none  [the longest x1 217 us: on_device(): input_total = lax.psum_scatter(term, 'row', scatter_dimension=0, tiled=True)]
    psum x2 -> x0, blocking collectives: 169 us -> none  [the longest x1 142 us: on_device(): lax.psum(jnp.dot(hidden_activation, down_adapter_squeeze, preferred_eleme...]
    all_gather x2 -> x0, waiting for transfers between devices: 153 us -> none  [the longest x1 79.7 us: on_device(): token_panel = lax.all_gather(tokens, 'row', axis=0, tiled=True)]
    pallas_call x0 -> x1, Pallas kernels: none -> 86.4 us  [on_device(): pl.pallas_call(kernel, out_shape=(out, out), in_specs=[vmem] * 2 + [anywh...]
    psum x1 -> x0, waiting for transfers between devices: 69.3 us -> none  [on_device(): gate_complete, up_complete = lax.psum((gate_portion, up_portion), 'col')]
    dot_general x18 -> x0, matrix products: 28.5 us -> none  [the longest x6 12 us: contract_last(): lax.dot_general(left, right, (((1,), (1,)), ((), ())), preferred_element_...]
    unnamed x22 -> x5, local copies, waits for them, and re-layouts: 0.52 us -> 8.03 us
  transfers between devices with their start and end apart: 5 -> 0, of which waited for: 5 -> 0; matrix products, arithmetic and copies ran while one was open for 2% -> 0% of each run, Pallas kernels for 0% -> 0%
where the time goes in v1:
time: 95.5 us; the launch traced here: 95 us
  Pallas kernels  86.4 us (90%)
  local copies, waits for them, and re-layouts  8.03 us (8%)
    pallas_call x1, Pallas kernels, on_device(): pl.pallas_call(kernel, out_shape=(out, out), in_specs=[vmem] * 2 + [anywh...  86.4 us
    unnamed x5, local copies, waits for them, and re-layouts  8.03 us

profile of v1, /device:TPU:32, one launch (start us, length us, event | category | flops | bytes accessed | tf_op | source)
XLA Modules:
  0.0 95.0 jit_solution(14611837411936373995)
XLA Ops:
  0.6 1.6 %copy.15.sd_ref = bf16[896,16]{1,0:T(8,128)(2,1)} copy(bf16[896,16]{0,1:T(8,128)(2,1)} %param.19) | data formatting | bytes 57344 | tf_op args[8]
  2.2 1.8 %copy.13.sg_ref = bf16[2048,16]{1,0:T(8,128)(2,1)} copy(bf16[2048,16]{0,1:T(8,128)(2,1)} %param.15) | data formatting | bytes 131072 | tf_op args[4]
  4.1 1.9 %copy.14.su_ref = bf16[2048,16]{1,0:T(8,128)(2,1)} copy(bf16[2048,16]{0,1:T(8,128)(2,1)} %param.17) | data formatting | bytes 131072 | tf_op args[6]
  5.9 86.4 %lora_swiglu.1 = (bf16[8,2048]{1,0:T(8,128)(2,1)}, bf16[8,2048]{1,0:T(8,128)(2,1)}) custom-call(bf16[8,2048]{1,0:T(8,128)(2,1)} %x_ref.1, bf16[8,2048]{1,0:T(8,128)(2,1)} %dy_ref.1, bf16[2048,896]{1,0:T(8,128)(2,1)} %wg_ref.1, bf16[2048,896]{1,0:T(8,128)(2,1)} %wu_ref.1, bf16[896,2048]{1,0:T(8,128)(2,1)} %wd_ref.1, bf16[2048,16]{1,0:T(8,128)(2,1)} %copy.13.sg_ref, ...), custom_call_target="tpu_custom_call" | custom-call | tf_op jit(solution)/shard_map/lora_swiglu/pallas_call | solution.py:330
  92.3 1.4 %copy.18 = bf16[8,2048]{1,0:T(8,128)(2,1)} copy(bf16[8,2048]{1,0:T(8,128)(2,1)} %get-tuple-element.4) | data formatting | bytes 65536
  93.6 1.4 %copy.19 = bf16[8,2048]{1,0:T(8,128)(2,1)} copy(bf16[8,2048]{1,0:T(8,128)(2,1)} %get-tuple-element.5) | data formatting | bytes 65536

commit v2 on v1

v2 whole, which is shorter than its diff:
```python
import jax
import jax.numpy as jnp
from jax import lax
from jax.experimental import pallas as pl
from jax.experimental.pallas import tpu as pltpu
from jax.sharding import PartitionSpec as P

MESH = pl.DeviceIdType.MESH
F32, BF16 = jnp.float32, jnp.bfloat16

NX, NCORE, NY, NZ = 4, 2, 4, 8
T, DC, FR, RANK = 256, 2048, 896, 16
FA = 1024
HALF, QUART = T // NCORE, T // NCORE // NX
TY = T // NY
CW = 512
NCH = DC // CW
ZGROUPS = ((0,), (1, 7), (2, 6), (3, 5, 4))
SCALE = 0.5


def nn(a, b):
    return jnp.dot(a, b, preferred_element_type=F32)


def nt(a, b):
    return lax.dot_general(a, b, (((1,), (1,)), ((), ())), preferred_element_type=F32)


def tn(a, b):
    return lax.dot_general(a, b, (((0,), (0,)), ((), ())), preferred_element_type=F32)


def split_inner(inner):
    top = inner.astype(BF16).astype(F32)
    lane = lax.broadcasted_iota(jnp.int32, inner.shape, 1)
    return (jnp.where(lane < RANK, top, inner - top) * SCALE).astype(BF16)


def kernel(
    x_ref, dy_ref, wg_ref, wu_ref, wd_ref, sg_ref, lg_ref, su_ref, lu_ref, sd_ref, ld_ref,
    mixed_ref, tg_ref,
    xin, wga, wua, wda, lga, lua, sda, sgt, sut, sdt,
    g, pan, acc, part, sib, own, xs, xr, act, mf, ms, ry, rp, zo, zs, zr,
    wsem, ss, rs,
):
    r, c = lax.axis_index("row"), lax.axis_index("col")
    y, z = r // NZ, r % NZ
    x, k = c // NCORE, c % NCORE

    def dev(dx=0, dk=0, dy=0, dz=0):
        return {
            "row": ((y + dy) % NY) * NZ + (z + dz) % NZ,
            "col": ((x + dx) % NX) * NCORE + (k + dk) % NCORE,
        }

    peers = (
        [dict(dz=d) for d in range(1, NZ)]
        + [dict(dy=d) for d in range(1, NY)]
        + [dict(dx=d) for d in range(1, NX)]
        + [dict(dk=1)]
    )
    barrier = pltpu.get_barrier_semaphore()
    for p in peers:
        pl.semaphore_signal(barrier, inc=1, device_id=dev(**p), device_id_type=MESH)

    loads = {}

    def load(name, i, src, dst):
        cp = pltpu.make_async_copy(src, dst, wsem.at[i])
        cp.start()
        loads[name] = cp

    load("x", 12, x_ref, xin.at[0])
    load("dy", 13, dy_ref, xin.at[1])
    loads["x"].wait()
    loads["dy"].wait()

    for a in range(2):
        v = xin[a].astype(F32)
        for h in range(2):
            q = DC // 4
            g[a, h, r] = jnp.concatenate(
                [v[:, 2 * h * q : (2 * h + 1) * q], v[:, (2 * h + 1) * q : (2 * h + 2) * q]], axis=0
            ).astype(BF16)

    pl.semaphore_wait(barrier, len(peers))

    recv_sems, send_sems = {}, {}

    def sem_of(ref, table, key):
        return ref.at[table.setdefault(key, len(table))]

    def send(src, dst, sent, key, **to):
        cp = pltpu.make_async_remote_copy(
            src_ref=src, dst_ref=dst, send_sem=sem_of(ss, send_sems, sent), recv_sem=sem_of(rs, recv_sems, key),
            device_id=dev(**to), device_id_type=MESH,
        )
        cp.start()

    def arrived(like, key):
        pltpu.make_async_remote_copy(
            src_ref=like, dst_ref=like, send_sem=ss.at[0], recv_sem=sem_of(rs, recv_sems, key),
            device_id=dev(dk=1), device_id_type=MESH,
        ).wait_recv()

    def all_sent(like, sent):
        pltpu.make_async_remote_copy(
            src_ref=like, dst_ref=like, send_sem=sem_of(ss, send_sems, sent), recv_sem=rs.at[0],
            device_id=dev(dk=1), device_id_type=MESH,
        ).wait_send()

    def block(a, h, dy, dz):
        return g.at[a, h, ((y + dy) % NY) * NZ + (z + dz) % NZ]

    def gather_z(a, h):
        b = block(a, h, 0, 0)
        for i, group in enumerate(ZGROUPS[1:]):
            for dz in group:
                send(b, b, ("g", a, h), ("gz", a, h, i + 1), dz=dz)

    def gather_y(a, h):
        for i, group in enumerate(ZGROUPS):
            if i:
                arrived(g.at[a, h, 0 : len(group)], ("gz", a, h, i))
            for dz in group:
                b = block(a, h, 0, -dz)
                send(b, b, ("g", a, h), ("gy", a, h, i), dy=(1, 3)[h])
                send(b, b, ("g", a, h), ("ge", a, h), dy=(3, 1)[h])

    def gather_forward(a, h):
        dy = (1, 3)[h]
        for i, group in enumerate(ZGROUPS):
            arrived(g.at[a, h, 0 : len(group)], ("gy", a, h, i))
            for dz in group:
                b = block(a, h, -dy, -dz)
                send(b, b, ("g", a, h), ("gf", a, h), dy=dy)

    def gather_end(a, h):
        arrived(g.at[a, h, 0:NZ], ("ge", a, h))
        arrived(g.at[a, h, 0:NZ], ("gf", a, h))
        for i in range(4):
            v = g[a, h, 8 * i : 8 * i + 8].astype(F32).reshape(8, 2, 8, DC // 4)
            rows = slice(64 * i, 64 * i + 64)
            pan[a, h, rows, 0 : DC // 4] = v[:, 0].reshape(64, DC // 4).astype(BF16)
            pan[a, h, rows, DC // 4 : DC // 2] = v[:, 1].reshape(64, DC // 4).astype(BF16)

    gather_z(0, 0)
    gather_z(0, 1)
    load("sg", 0, sg_ref, sgt)
    load("su", 1, su_ref, sut)
    load("wg", 2, wg_ref, wga.at[:, 0:FR])
    load("wu", 3, wu_ref, wua.at[:, 0:FR])
    load("lg0", 4, lg_ref, lga.at[0:RANK])
    load("lg1", 5, lg_ref, lga.at[RANK : 2 * RANK])
    load("lu0", 6, lu_ref, lua.at[0:RANK])
    load("lu1", 7, lu_ref, lua.at[RANK : 2 * RANK])
    load("wd", 8, wd_ref, wda.at[0:FR])
    load("ld0", 9, ld_ref, wda.at[FR : FR + RANK])
    load("ld1", 10, ld_ref, wda.at[FR + RANK : FR + 2 * RANK])
    load("sd", 11, sd_ref, sdt)

    rows16 = lax.broadcasted_iota(jnp.int32, (RANK, 128), 0)
    lanes = lax.broadcasted_iota(jnp.int32, (RANK, 128), 1)
    twice = ((lanes % RANK == rows16) & (lanes < 2 * RANK)).astype(F32).astype(BF16)
    for name, src, dst in (("sg", sgt, wga), ("su", sut, wua)):
        loads[name].wait()
        dst[:, FR:FA] = tn(src[...], twice).astype(BF16)
    for dst in (lga, lua):
        dst[2 * RANK : 128] = jnp.zeros((128 - 2 * RANK, FR), BF16)
    wda[FR + 2 * RANK : FA] = jnp.zeros((FA - FR - 2 * RANK, DC), BF16)

    gather_y(0, 0)
    gather_y(0, 1)
    gather_z(1, 0)
    gather_z(1, 1)
    gather_forward(0, 0)
    gather_forward(0, 1)
    loads["sd"].wait()
    sda[...] = tn(sdt[...], twice).astype(BF16)
    gather_y(1, 0)
    gather_y(1, 1)
    for name in ("wg", "wu", "lg0", "lg1", "lu0", "lu1"):
        loads[name].wait()

    other = pl.multiple_of((1 - k) * HALF, HALF)
    mine = pl.multiple_of(k * HALF, HALF)
    myrow = pl.multiple_of(k * HALF + x * QUART, QUART)

    def sum_cores(a):
        send(part.at[a, pl.ds(other, HALF)], sib.at[a], "sib", ("sib", a), dk=1)

    def sum_x(a):
        arrived(sib.at[a], ("sib", a))
        for q in range(NX):
            rows = pl.ds(pl.multiple_of(mine + q * QUART, QUART), QUART)
            v = part[a, rows, :] + sib[a, q * QUART : (q + 1) * QUART, :]
            own[a, q] = v
            xs[a, q] = v.astype(BF16)
        for dx in (1, 3, 2):
            send(xs.at[a, (x + dx) % NX], xr.at[a, dx - 1], "xr", ("xr", a), dx=dx)

    def total_x(a):
        arrived(xr.at[a], ("xr", a))
        return own[a, x] + xr[a, 0].astype(F32) + xr[a, 1].astype(F32) + xr[a, 2].astype(F32)

    low, high = slice(0, DC // 2), slice(DC // 2, DC)
    tiles = [slice(256 * j, 256 * (j + 1)) for j in range(4)]

    def forward_low(a, w):
        for t in tiles:
            acc[a, :, t] = nn(pan[0, 0], w[low, t])

    def forward_high(a, w, lift):
        o = acc[a, :, tiles[3]] + nn(pan[0, 1], w[high, tiles[3]])
        sel = split_inner(o[:, 128:256])
        part[a, :, 768:FR] = o[:, 0:128] + nn(sel, lift[:, 768:FR])
        for t in tiles[:3]:
            part[a, :, t] = acc[a, :, t] + nn(pan[0, 1], w[high, t]) + nn(sel, lift[:, t])

    gather_end(0, 0)
    forward_low(0, wga)
    forward_low(1, wua)
    gather_end(0, 1)
    forward_high(0, wga, lga)
    sum_cores(0)
    forward_high(1, wua, lua)
    sum_cores(1)
    gather_forward(1, 0)
    sum_x(0)
    gather_forward(1, 1)
    sum_x(1)

    for name in ("wd", "ld0", "ld1"):
        loads[name].wait()
    gather_end(1, 0)
    for t in tiles:
        acc[0, :, t] = nt(pan[1, 0], wda[t, low])
    gather_end(1, 1)
    o = acc[0, :, tiles[3]] + nt(pan[1, 1], wda[tiles[3], high])
    sel = split_inner(o[:, 128:256])
    part[2, :, 768:FR] = o[:, 0:128] + nt(sel, sda[768:FR, :])
    for t in tiles[:3]:
        part[2, :, t] = acc[0, :, t] + nt(pan[1, 1], wda[t, high]) + nt(sel, sda[t, :])
    sum_cores(2)

    def spread(a):
        b = act.at[a, pl.ds(myrow, QUART), 0:FR]
        for dx in (1, 3, 2):
            send(b, b, ("a", a), ("ax", a), dx=dx)
        send(b, b, ("a", a), ("ak", a), dk=1)

    def spread_on(a):
        arrived(act.at[a, 0 : 3 * QUART, 0:FR], ("ax", a))
        for dx in (1, 3, 2):
            rows = pl.multiple_of(k * HALF + ((x - dx) % NX) * QUART, QUART)
            b = act.at[a, pl.ds(rows, QUART), 0:FR]
            send(b, b, ("a", a), ("ak", a), dk=1)

    def spread_end(a):
        arrived(act.at[a, 0:HALF, 0:FR], ("ak", a))

    gate = total_x(0)
    up = total_x(1)
    sigmoid = jax.nn.sigmoid(gate)
    act[0, pl.ds(myrow, QUART), 0:FR] = (gate * sigmoid * up).astype(BF16)
    spread(0)

    def at_y(d):
        return pl.ds(pl.multiple_of(((y + d) % NY) * TY, TY), TY)

    def parts_of(j):
        return slice(CW * j, CW * j + CW // 2), slice(CW * j + CW // 2, CW * (j + 1))

    def y_send(a, j, value):
        first, rest = parts_of(j)
        cols = slice(CW * j, CW * (j + 1))
        mf[a, :, cols] = value
        ms[a, :, cols] = value.astype(BF16)
        send(ms.at[a, at_y(2), first], rp.at[a, j, 0], ("y", a), ("rp", a, j), dy=1)
        send(ms.at[a, at_y(2), rest], rp.at[a, j, 1], ("y", a), ("rp", a, j), dy=3)
        send(ms.at[a, at_y(1), rest], ry.at[a, 0, :, rest], ("y", a), ("ry", a, j), dy=1)
        send(ms.at[a, at_y(3), first], ry.at[a, 1, :, first], ("y", a), ("ry", a, j), dy=3)

    def y_relay(a, j):
        first, rest = parts_of(j)
        arrived(rp.at[a, j], ("rp", a, j))
        for i, (dy, cols) in enumerate(((1, first), (3, rest))):
            ms[a, at_y(dy), cols] = (mf[a, at_y(dy), cols] + rp[a, j, i].astype(F32)).astype(BF16)
            send(ms.at[a, at_y(dy), cols], ry.at[a, i, :, cols], ("y", a), ("ry", a, j), dy=dy)

    def z_send(a, j):
        cols = slice(CW * j, CW * (j + 1))
        arrived(ry.at[a, :, :, cols], ("ry", a, j))
        v = mf[a, at_y(0), cols] + ry[a, 0, :, cols].astype(F32) + ry[a, 1, :, cols].astype(F32)
        v = v.reshape(NZ, 8, CW)
        v = jnp.concatenate([v[:, :, : CW // 2], v[:, :, CW // 2 :]], axis=1)
        zo[a, j] = v
        zs[a, j] = v.astype(BF16)
        for dz in (4, 3, 5, 2, 6, 1, 7):
            send(zs.at[a, j, (z + dz) % NZ], zr.at[a, j, dz - 1], ("z", a), ("zr", a, j), dz=dz)

    def z_end(a, j, out_ref):
        v = zo[a, j, z]
        arrived(zr.at[a, j], ("zr", a, j))
        for dz in range(1, NZ):
            v = v + zr[a, j, dz - 1].astype(F32)
        first, rest = parts_of(j)
        out_ref[:, first] = v[0:8].astype(BF16)
        out_ref[:, rest] = v[8:16].astype(BF16)

    def down(j):
        y_send(0, j, nn(act[0], wda[:, CW * j : CW * (j + 1)]))

    def back(j):
        rows = slice(CW * j, CW * (j + 1))
        y_send(1, j, nt(act[1], wga[rows, :]) + nt(act[2], wua[rows, :]))

    sum_x(2)
    spread_on(0)
    spread_end(0)
    act[0, :, FR:FA] = split_inner(nn(act[0, :, 0:FR], sda[...]))
    down(0)
    down(1)

    hidden_gradient = total_x(2)
    act[1, pl.ds(myrow, QUART), 0:FR] = (
        hidden_gradient * up * sigmoid * (1.0 + gate * (1.0 - sigmoid))
    ).astype(BF16)
    act[2, pl.ds(myrow, QUART), 0:FR] = (hidden_gradient * gate * sigmoid).astype(BF16)
    spread(1)
    spread(2)

    y_relay(0, 0)
    down(2)
    y_relay(0, 1)
    down(3)
    y_relay(0, 2)
    spread_on(1)
    z_send(0, 0)
    y_relay(0, 3)
    spread_on(2)
    z_send(0, 1)
    spread_end(1)
    act[1, :, FR:FA] = split_inner(nt(act[1, :, 0:FR], lga[...]))
    spread_end(2)
    act[2, :, FR:FA] = split_inner(nt(act[2, :, 0:FR], lua[...]))
    back(0)
    z_send(0, 2)
    back(1)
    y_relay(1, 0)
    z_send(0, 3)
    back(2)
    y_relay(1, 1)
    back(3)
    y_relay(1, 2)
    z_send(1, 0)
    y_relay(1, 3)
    z_send(1, 1)
    for j in range(NCH):
        z_end(0, j, mixed_ref)
    z_send(1, 2)
    z_send(1, 3)
    for j in range(NCH):
        z_end(1, j, tg_ref)
    for a in range(2):
        for h in range(2):
            all_sent(g.at[a, h, 0:31], ("g", a, h))
    all_sent(sib, "sib")
    all_sent(xr, "xr")
    for a in range(3):
        all_sent(act.at[a, 0 : 7 * QUART, 0:FR], ("a", a))
    for a in range(2):
        all_sent(ms.at[a, 0 : 3 * TY], ("y", a))
        all_sent(zr.at[a], ("z", a))


def on_device(tokens, gate_w, up_w, down_w, gate_s, gate_l, up_s, up_l, down_s, down_l, cotangent):
    vmem = pl.BlockSpec(memory_space=pltpu.VMEM)
    anywhere = pl.BlockSpec(memory_space=pl.ANY)
    out = jax.ShapeDtypeStruct((T // NY // NZ, DC), BF16)
    return pl.pallas_call(
        kernel,
        out_shape=(out, out),
        in_specs=[anywhere] * 11,
        out_specs=(vmem, vmem),
        scratch_shapes=[
            pltpu.VMEM((2, T // NY // NZ, DC), BF16),
            pltpu.VMEM((DC, FA), BF16),
            pltpu.VMEM((DC, FA), BF16),
            pltpu.VMEM((FA, DC), BF16),
            pltpu.VMEM((128, FR), BF16),
            pltpu.VMEM((128, FR), BF16),
            pltpu.VMEM((FR, 128), BF16),
            pltpu.VMEM((RANK, DC), BF16),
            pltpu.VMEM((RANK, DC), BF16),
            pltpu.VMEM((RANK, FR), BF16),
            pltpu.VMEM((2, 2, NY * NZ, 16, DC // 4), BF16),
            pltpu.VMEM((2, 2, T, DC // 2), BF16),
            pltpu.VMEM((2, T, FA), F32),
            pltpu.VMEM((3, T, FR), F32),
            pltpu.VMEM((3, HALF, FR), F32),
            pltpu.VMEM((3, NX, QUART, FR), F32),
            pltpu.VMEM((3, NX, QUART, FR), BF16),
            pltpu.VMEM((3, NX - 1, QUART, FR), BF16),
            pltpu.VMEM((3, T, FA), BF16),
            pltpu.VMEM((2, T, DC), F32),
            pltpu.VMEM((2, T, DC), BF16),
            pltpu.VMEM((2, 2, TY, DC), BF16),
            pltpu.VMEM((2, NCH, 2, TY, CW // 2), BF16),
            pltpu.VMEM((2, NCH, NZ, 16, CW // 2), F32),
            pltpu.VMEM((2, NCH, NZ, 16, CW // 2), BF16),
            pltpu.VMEM((2, NCH, NZ - 1, 16, CW // 2), BF16),
            pltpu.SemaphoreType.DMA((14,)),
            pltpu.SemaphoreType.DMA((13,)),
            pltpu.SemaphoreType.DMA((72,)),
        ],
        compiler_params=pltpu.CompilerParams(
            collective_id=0, has_side_effects=True, vmem_limit_bytes=58 * 2**20
        ),
        name="lora_swiglu",
    )(tokens, cotangent, gate_w, up_w, down_w, gate_s.T, gate_l, up_s.T, up_l, down_s.T, down_l)


def solution(mesh):
    placed = (
        P("row", "col"),
        P("col", "row"),
        P("col", "row"),
        P("row", "col"),
        P("col", None),
        P(None, "row"),
        P("col", None),
        P(None, "row"),
        P("row", None),
        P(None, "col"),
        P("row", "col"),
    )
    return jax.shard_map(
        on_device,
        mesh=mesh,
        in_specs=placed,
        out_specs=(P("row", "col"), P("row", "col")),
        check_vma=False,
    )
```

time: 95.5 us -> 78.9 us (0.83)
  Pallas kernels: 86.4 us -> 74.9 us
  local copies, waits for them, and re-layouts: 8.03 us -> 2.75 us
    pallas_call x1, Pallas kernels: 86.4 us -> 74.9 us  [on_device(): pl.pallas_call(kernel, out_shape=(out, out), in_specs=[anywhere] * 11, ou...]
    unnamed x5 -> x2, local copies, waits for them, and re-layouts: 8.03 us -> 2.75 us
where the time goes in v2:
time: 78.9 us; the launch traced here: 78.3 us
  Pallas kernels  74.9 us (95%)
  local copies, waits for them, and re-layouts  2.75 us (3%)
    pallas_call x1, Pallas kernels, on_device(): pl.pallas_call(kernel, out_shape=(out, out), in_specs=[anywhere] * 11, ou...  74.9 us
    unnamed x2, local copies, waits for them, and re-layouts  2.75 us

profile of v2, /device:TPU:32, one launch (start us, length us, event | category | flops | bytes accessed | tf_op | source)
XLA Modules:
  0.0 78.3 jit_solution(6240466123551521991)
XLA Ops:
  0.6 74.9 %lora_swiglu.1 = (bf16[8,2048]{1,0:T(8,128)(2,1)}, bf16[8,2048]{1,0:T(8,128)(2,1)}) custom-call(bf16[8,2048]{1,0:T(8,128)(2,1)} %x_ref.1, bf16[8,2048]{1,0:T(8,128)(2,1)} %dy_ref.1, bf16[2048,896]{1,0:T(8,128)(2,1)} %wg_ref.1, bf16[2048,896]{1,0:T(8,128)(2,1)} %wu_ref.1, bf16[896,2048]{1,0:T(8,128)(2,1)} %wd_ref.1, bf16[16,2048]{1,0:T(8,128)(2,1)} %bitcast.3, ...), custom_call_target="tpu_custom_call" | custom-call | tf_op jit(solution)/shard_map/lora_swiglu/pallas_call | solution.py:382
  75.6 1.4 %copy.15 = bf16[8,2048]{1,0:T(8,128)(2,1)} copy(bf16[8,2048]{1,0:T(8,128)(2,1)} %get-tuple-element.4) | data formatting | bytes 65536
  76.9 1.4 %copy.16 = bf16[8,2048]{1,0:T(8,128)(2,1)} copy(bf16[8,2048]{1,0:T(8,128)(2,1)} %get-tuple-element.5) | data formatting | bytes 65536

commit v3 on v2

--- a/solution.py
+++ b/solution.py
@@ -17,6 +17,7 @@
 NCH = DC // CW
 ZGROUPS = ((0,), (1, 7), (2, 6), (3, 5, 4))
 SCALE = 0.5
+RS_DIRECT = ((1, 2), (1, 3))
 
 
 def nn(a, b):
@@ -273,26 +274,38 @@
         return slice(CW * j, CW * j + CW // 2), slice(CW * j + CW // 2, CW * (j + 1))
 
     def y_send(a, j, value):
-        first, rest = parts_of(j)
-        cols = slice(CW * j, CW * (j + 1))
-        mf[a, :, cols] = value
-        ms[a, :, cols] = value.astype(BF16)
-        send(ms.at[a, at_y(2), first], rp.at[a, j, 0], ("y", a), ("rp", a, j), dy=1)
-        send(ms.at[a, at_y(2), rest], rp.at[a, j, 1], ("y", a), ("rp", a, j), dy=3)
-        send(ms.at[a, at_y(1), rest], ry.at[a, 0, :, rest], ("y", a), ("ry", a, j), dy=1)
-        send(ms.at[a, at_y(3), first], ry.at[a, 1, :, first], ("y", a), ("ry", a, j), dy=3)
+        mf[a, :, CW * j : CW * (j + 1)] = value
+        for h, part_cols in enumerate(parts_of(0)):
+            ms[a, 2 * j + h] = value[:, part_cols].astype(BF16)
+        first, rest = ms.at[a, 2 * j], ms.at[a, 2 * j + 1]
+        if (a, j) in RS_DIRECT:
+            for h in range(2):
+                for i, dy in enumerate((1, 3)):
+                    send(ms.at[a, 2 * j + h, at_y(dy)], ry.at[a, j, i, h], ("y", a), ("ry", a, j), dy=dy)
+            for h in range(2):
+                send(ms.at[a, 2 * j + h, at_y(2)], rp.at[a, j, h], ("y", a), ("rp", a, j), dy=2)
+            return
+        send(first.at[at_y(2)], rp.at[a, j, 0], ("y", a), ("rp", a, j), dy=1)
+        send(rest.at[at_y(2)], rp.at[a, j, 1], ("y", a), ("rp", a, j), dy=3)
+        send(rest.at[at_y(1)], ry.at[a, j, 0, 1], ("y", a), ("ry", a, j), dy=1)
+        send(first.at[at_y(3)], ry.at[a, j, 1, 0], ("y", a), ("ry", a, j), dy=3)
 
     def y_relay(a, j):
-        first, rest = parts_of(j)
+        if (a, j) in RS_DIRECT:
+            return
         arrived(rp.at[a, j], ("rp", a, j))
-        for i, (dy, cols) in enumerate(((1, first), (3, rest))):
-            ms[a, at_y(dy), cols] = (mf[a, at_y(dy), cols] + rp[a, j, i].astype(F32)).astype(BF16)
-            send(ms.at[a, at_y(dy), cols], ry.at[a, i, :, cols], ("y", a), ("ry", a, j), dy=dy)
+        for i, (dy, cols) in enumerate(zip((1, 3), parts_of(j))):
+            b = ms.at[a, 2 * j + i, at_y(dy)]
+            b[...] = (mf[a, at_y(dy), cols] + rp[a, j, i].astype(F32)).astype(BF16)
+            send(b, ry.at[a, j, i, i], ("y", a), ("ry", a, j), dy=dy)
 
     def z_send(a, j):
-        cols = slice(CW * j, CW * (j + 1))
-        arrived(ry.at[a, :, :, cols], ("ry", a, j))
-        v = mf[a, at_y(0), cols] + ry[a, 0, :, cols].astype(F32) + ry[a, 1, :, cols].astype(F32)
+        arrived(ry.at[a, j], ("ry", a, j))
+        w = ry[a, j, 0].astype(F32) + ry[a, j, 1].astype(F32)
+        if (a, j) in RS_DIRECT:
+            arrived(rp.at[a, j], ("rp", a, j))
+            w = w + rp[a, j].astype(F32)
+        v = mf[a, at_y(0), CW * j : CW * (j + 1)] + jnp.concatenate([w[0], w[1]], axis=1)
         v = v.reshape(NZ, 8, CW)
         v = jnp.concatenate([v[:, :, : CW // 2], v[:, :, CW // 2 :]], axis=1)
         zo[a, j] = v
@@ -318,10 +331,6 @@
 
     sum_x(2)
     spread_on(0)
-    spread_end(0)
-    act[0, :, FR:FA] = split_inner(nn(act[0, :, 0:FR], sda[...]))
-    down(0)
-    down(1)
 
     hidden_gradient = total_x(2)
     act[1, pl.ds(myrow, QUART), 0:FR] = (
@@ -331,15 +340,19 @@
     spread(1)
     spread(2)
 
+    spread_end(0)
+    act[0, :, FR:FA] = split_inner(nn(act[0, :, 0:FR], sda[...]))
+    down(0)
+    down(1)
+    down(2)
+    spread_on(1)
     y_relay(0, 0)
-    down(2)
+    down(3)
+    spread_on(2)
     y_relay(0, 1)
-    down(3)
     y_relay(0, 2)
-    spread_on(1)
     z_send(0, 0)
     y_relay(0, 3)
-    spread_on(2)
     z_send(0, 1)
     spread_end(1)
     act[1, :, FR:FA] = split_inner(nt(act[1, :, 0:FR], lga[...]))
@@ -371,15 +384,20 @@
     for a in range(3):
         all_sent(act.at[a, 0 : 7 * QUART, 0:FR], ("a", a))
     for a in range(2):
-        all_sent(ms.at[a, 0 : 3 * TY], ("y", a))
+        all_sent(ms.at[a, 0:6], ("y", a))
         all_sent(zr.at[a], ("z", a))
+
+
+def hand_over(mixed_ref, tg_ref, mixed_out, tg_out):
+    mixed_out[...] = mixed_ref[...]
+    tg_out[...] = tg_ref[...]
 
 
 def on_device(tokens, gate_w, up_w, down_w, gate_s, gate_l, up_s, up_l, down_s, down_l, cotangent):
     vmem = pl.BlockSpec(memory_space=pltpu.VMEM)
     anywhere = pl.BlockSpec(memory_space=pl.ANY)
     out = jax.ShapeDtypeStruct((T // NY // NZ, DC), BF16)
-    return pl.pallas_call(
+    mixed, gradient = pl.pallas_call(
         kernel,
         out_shape=(out, out),
         in_specs=[anywhere] * 11,
@@ -405,8 +423,8 @@
             pltpu.VMEM((3, NX - 1, QUART, FR), BF16),
             pltpu.VMEM((3, T, FA), BF16),
             pltpu.VMEM((2, T, DC), F32),
-            pltpu.VMEM((2, T, DC), BF16),
-            pltpu.VMEM((2, 2, TY, DC), BF16),
+            pltpu.VMEM((2, 2 * NCH, T, CW // 2), BF16),
+            pltpu.VMEM((2, NCH, 2, 2, TY, CW // 2), BF16),
             pltpu.VMEM((2, NCH, 2, TY, CW // 2), BF16),
             pltpu.VMEM((2, NCH, NZ, 16, CW // 2), F32),
             pltpu.VMEM((2, NCH, NZ, 16, CW // 2), BF16),
@@ -420,6 +438,9 @@
         ),
         name="lora_swiglu",
     )(tokens, cotangent, gate_w, up_w, down_w, gate_s.T, gate_l, up_s.T, up_l, down_s.T, down_l)
+    return pl.pallas_call(
+        hand_over, out_shape=(out, out), in_specs=[vmem] * 2, out_specs=(vmem, vmem), name="hand_over"
+    )(mixed, gradient)
 
 
 def solution(mesh):

time: 78.9 us -> 76.9 us (0.975)
  local copies, waits for them, and re-layouts: 2.75 us -> 0 us
  Pallas kernels: 74.9 us -> 76.1 us
    unnamed x2 -> x0, local copies, waits for them, and re-layouts: 2.75 us -> none
    pallas_call x0 -> x1, Pallas kernels: none -> 1.4 us  [on_device(): pl.pallas_call(hand_over, out_shape=(out, out), in_specs=[vmem] * 2, out_...]
where the time goes in v3:
time: 76.9 us; the launch traced here: 76.7 us
  Pallas kernels  76.1 us (99%)
    pallas_call x1, Pallas kernels, on_device(): pl.pallas_call(kernel, out_shape=(out, out), in_specs=[anywhere] * 11, ou...  74.7 us

profile of v3, /device:TPU:32, one launch (start us, length us, event | category | flops | bytes accessed | tf_op | source)
XLA Modules:
  0.0 76.7 jit_solution(10877286319711724352)
XLA Ops:
  0.6 74.7 %lora_swiglu.1 = (bf16[8,2048]{1,0:T(8,128)(2,1)}, bf16[8,2048]{1,0:T(8,128)(2,1)}) custom-call(bf16[8,2048]{1,0:T(8,128)(2,1)} %x_ref.1, bf16[8,2048]{1,0:T(8,128)(2,1)} %dy_ref.1, bf16[2048,896]{1,0:T(8,128)(2,1)} %wg_ref.1, bf16[2048,896]{1,0:T(8,128)(2,1)} %wu_ref.1, bf16[896,2048]{1,0:T(8,128)(2,1)} %wd_ref.1, bf16[16,2048]{1,0:T(8,128)(2,1)} %bitcast.3, ...), custom_call_target="tpu_custom_call" | custom-call | tf_op jit(solution)/shard_map/lora_swiglu/pallas_call | solution.py:400
  75.3 1.4 %hand_over.1 = (bf16[8,2048]{1,0:T(8,128)(2,1)}, bf16[8,2048]{1,0:T(8,128)(2,1)}) custom-call(bf16[8,2048]{1,0:T(8,128)(2,1)} %get-tuple-element.4.mixed_ref, bf16[8,2048]{1,0:T(8,128)(2,1)} %get-tuple-element.5.tg_ref), custom_call_target="tpu_custom_call" | custom-call | tf_op jit(solution)/shard_map/hand_over/pallas_call | solution.py:441

commit v4 on v3

--- a/solution.py
+++ b/solution.py
@@ -227,10 +227,10 @@
     sum_cores(0)
     forward_high(1, wua, lua)
     sum_cores(1)
+    sum_x(0)
+    sum_x(1)
     gather_forward(1, 0)
-    sum_x(0)
     gather_forward(1, 1)
-    sum_x(1)
 
     for name in ("wd", "ld0", "ld1"):
         loads[name].wait()

time: 76.9 us -> 77.2 us (level)
  no operation moved by 1% of the time
where the time goes in v4:
time: 77.2 us; the launch traced here: 77 us
  Pallas kernels  76.4 us (99%)
    pallas_call x1, Pallas kernels, on_device(): pl.pallas_call(kernel, out_shape=(out, out), in_specs=[anywhere] * 11, ou...  74.9 us

profile of v4, /device:TPU:32, one launch (start us, length us, event | category | flops | bytes accessed | tf_op | source)
XLA Modules:
  0.0 77.0 jit_solution(331267874101683610)
XLA Ops:
  0.6 74.9 %lora_swiglu.1 = (bf16[8,2048]{1,0:T(8,128)(2,1)}, bf16[8,2048]{1,0:T(8,128)(2,1)}) custom-call(bf16[8,2048]{1,0:T(8,128)(2,1)} %x_ref.1, bf16[8,2048]{1,0:T(8,128)(2,1)} %dy_ref.1, bf16[2048,896]{1,0:T(8,128)(2,1)} %wg_ref.1, bf16[2048,896]{1,0:T(8,128)(2,1)} %wu_ref.1, bf16[896,2048]{1,0:T(8,128)(2,1)} %wd_ref.1, bf16[16,2048]{1,0:T(8,128)(2,1)} %bitcast.3, ...), custom_call_target="tpu_custom_call" | custom-call | tf_op jit(solution)/shard_map/lora_swiglu/pallas_call | solution.py:400
  75.6 1.4 %hand_over.1 = (bf16[8,2048]{1,0:T(8,128)(2,1)}, bf16[8,2048]{1,0:T(8,128)(2,1)}) custom-call(bf16[8,2048]{1,0:T(8,128)(2,1)} %get-tuple-element.4.mixed_ref, bf16[8,2048]{1,0:T(8,128)(2,1)} %get-tuple-element.5.tg_ref), custom_call_target="tpu_custom_call" | custom-call | tf_op jit(solution)/shard_map/hand_over/pallas_call | solution.py:441
